TPU v7x, 32 devices: a whole 2x2x4 slice. The times are simulated.
32 devices in a mesh: row: 8 (over y, x, core), seg: 4 (over z).
Axes of the slice: x: 2, y: 2, z: 4, core: 2. Of those that a mesh axis runs over, the one named last changes fastest.
Arguments:
- tokens: bfloat16 [64, 1024, 768], P('row', 'seg'), may hold values from -6 to 6
- doc_ids: int32 [64, 8], P('row'), may hold values from 0 to 7, as said below
- w_qkv: bfloat16 [2, 768, 2304], replicated, may hold values from -0.21875 to 0.21875
- w_out: bfloat16 [2, 768, 768], replicated, may hold values from -0.875 to 0.875
- w_up: bfloat16 [2, 768, 3072], replicated, may hold values from -0.21875 to 0.21875
- w_down: bfloat16 [2, 3072, 768], replicated, may hold values from -0.109375 to 0.109375
- biases: bfloat16 [2, 6, 768], replicated, may hold values from -1 to 1
- gains: bfloat16 [2, 2, 768], replicated, may hold values from 0.5 to 1.5
- b_up: bfloat16 [2, 3072], replicated, may hold values from -1 to 1
- pos_table: bfloat16 [8, 768], replicated, may hold values from -3 to 3
- cotangent: bfloat16 [64, 1024, 768], P('row', 'seg'), may hold values from -6 to 6
Outputs:
- output: bfloat16 [64, 1024, 768], P('row', 'seg')
- grad_tokens: float32 [64, 1024, 768], P('row', 'seg')
- grad_w_qkv: float32 [1536, 2304], P(('row', 'seg'))
- grad_w_out: float32 [1536, 768], P(('row', 'seg'))
- grad_w_up: float32 [1536, 3072], P(('row', 'seg'))
- grad_w_down: float32 [6144, 768], P(('row', 'seg'))
- grad_biases: float32 [9216], P(('row', 'seg'))
- grad_gains: float32 [3072], P(('row', 'seg'))
- grad_b_up: float32 [6144], P(('row', 'seg'))
- grad_pos_table: float32 [6144], P(('row', 'seg'))
Inputs may be any that keep to these rules, and one draw needn't show every extreme that they name: `doc_ids`: in each row the ids start at 0 and rise by 0 or 1 from one segment to the next; among rows 8 * g to 8 * g + 7 at least one row is a single document; where 8 is 2 or more, some row among the first 8 rows has every segment in a document of its own.
All inputs are finite; a program needn't handle non-finite values.
Results may differ from a plain program's by a relative error of at most 0.02.
Values may be sent and summed in bfloat16 or wider, within the bound.
A program may use at most 256 MiB of HBM per device.

v0:
```python
import functools

import jax
import jax.numpy as jnp
from jax import lax
from jax.experimental import pallas as pl
from jax.experimental.pallas import tpu as pltpu
from jax.sharding import PartitionSpec as P


HDIM = 64
SEGLEN = 128
LANES = 128
GROUP = 2 * LANES
EPSILON = 1e-05
GELU_A = 0.7978845608028654
GELU_B = 0.044715 * GELU_A
F32, BF16 = jnp.float32, jnp.bfloat16


def mm(a, b):
    return lax.dot_general(a, b, (((1,), (0,)), ((), ())), preferred_element_type=F32)


def mm_nt(a, b):
    return lax.dot_general(a, b, (((1,), (1,)), ((), ())), preferred_element_type=F32)


def mm_tn(a, b):
    return lax.dot_general(a, b, (((0,), (0,)), ((), ())), preferred_element_type=F32)


def low_lanes(shape):
    return lax.broadcasted_iota(jnp.int32, shape, 1) < HDIM


def stack_heads(pair):
    keep = low_lanes(pair.shape)
    zero = jnp.zeros_like(pair)
    return jnp.concatenate([jnp.where(keep, pair, zero), jnp.where(keep, zero, pair)], axis=0)


def pair_lanes(half):
    return [slice(part * GROUP + half * LANES, part * GROUP + (half + 1) * LANES) for part in range(3)]


def norm_stats(values):
    centered = values - jnp.mean(values, axis=-1, keepdims=True)
    variance = jnp.mean(centered * centered, axis=-1, keepdims=True)
    rstd = lax.rsqrt(variance + EPSILON)
    return centered * rstd, rstd


def gelu_both(u):
    u = u.astype(BF16)
    square = u * u
    bend = GELU_B * square
    half = 0.5 * jnp.tanh(u * (GELU_A + bend))
    gate = half + 0.5
    hidden = u * gate
    slope = gate + hidden * (0.5 - half) * (2.0 * GELU_A + 6.0 * bend)
    return hidden, slope


def norm_back(grad, gain, normal, rstd):
    scaled = grad * gain
    a = jnp.mean(scaled, axis=-1, keepdims=True)
    b = jnp.mean(scaled * normal, axis=-1, keepdims=True)
    return (scaled - a - normal * b) * rstd


OUTS = 13
NEGATIVE = -1000000000.0
MESH = pl.DeviceIdType.MESH


def turned(values):
    return values.astype(F32).T.astype(BF16)


def places(docs, rows, own, kinds):
    lines, segments = docs.shape
    here = own // lines
    count = 2 * rows

    def spread(width, axis):
        return lax.broadcasted_iota(jnp.int32, (count, width), axis)

    def line_of(at):
        return lax.shift_right_logical(at & (own - 1), here.bit_length() - 1)

    in_line = line_of(spread(lines, 0)) == spread(lines, 1)
    row_docs = mm(in_line.astype(BF16), docs.astype(F32).astype(BF16))
    at = spread(segments, 0) & (rows - 1)
    segment = lax.shift_right_logical(at, own.bit_length() - 1) * here + (at & (here - 1))
    across = spread(segments, 1)
    doc = jnp.sum(jnp.where(across == segment, row_docs, 0.0), axis=1, keepdims=True)
    start = jnp.min(jnp.where(row_docs == doc, across.astype(F32), float(segments)), axis=1, keepdims=True)
    place = segment[:, 0:1].astype(F32) - start
    onehot = (place == spread(kinds, 1).astype(F32))[:rows].astype(F32)
    key = doc + segments * line_of(spread(1, 0)).astype(F32)
    keys_across = jnp.broadcast_to(key, (count, max(rows, LANES))).T[:rows]
    return onehot, key[:rows] == keys_across


def cross_part(me, doc_ref, table_ref, bias_ref, gain_ref, bup_ref, outs, writes, weights, copies, scratch, ff_chunk):
    (
        ccls_ref, gcls_ref, sums_ref, bsums_ref, gpos_ref, xt_ref, mixedt_ref, firstt_ref, hiddent_ref,
        gqkv_ref, gbranch_ref, ginner_ref, gsecond_ref,
    ) = outs
    wqkv, wout, wup, wdown = weights
    qkv_ref, probs_ref, mixed_ref, slope_ref, whole_ref = scratch
    own, width = ccls_ref.shape
    rows = whole_ref.shape[1]
    inners = wup.shape[1]
    bias = bias_ref[...].astype(F32)[:, 1]
    gain = gain_ref[1].astype(F32)
    up_bias = bup_ref[1:2, :].astype(F32)
    onehot, allowed = places(doc_ref[...], rows, own, table_ref.shape[0])
    embed = mm(onehot.astype(BF16), table_ref[...])
    x = (whole_ref[0] + embed).astype(BF16)
    gy = whole_ref[1]
    xt_ref[...] = turned(x)
    copies[0].wait()
    for part in range(3):
        cols = slice(part * width, (part + 1) * width)
        out = mm(x, wqkv[:, cols])
        if part == 0:
            out = out + bias[0:1]
        if part == 2:
            out = out + bias[1:2]
        qkv_ref[:, cols] = out.astype(BF16)
    low = low_lanes((rows, LANES))
    pairs = range(width // LANES)
    lanes = [[slice(part * width + pair * LANES, part * width + (pair + 1) * LANES) for part in range(3)] for pair in pairs]
    scores = [
        jnp.where(allowed, mm_nt(qkv_ref[:, at[1]], stack_heads(qkv_ref[:, at[0]] * HDIM**-0.5)), NEGATIVE) for at in lanes
    ]
    pt = []
    for pair in pairs:
        e = jnp.exp(scores[pair] - jnp.max(scores[pair], axis=0, keepdims=True))
        p = e * (1.0 / jnp.sum(e, axis=0, keepdims=True))
        probs_ref[pair] = p
        pt.append(p.T.astype(BF16))
    for pair, at in enumerate(lanes):
        v = qkv_ref[:, at[2]]
        mixed_ref[:, at[0]] = jnp.where(low, mm(pt[pair][:rows], v), mm(pt[pair][rows:], v)).astype(BF16)
    copies[1].wait()
    mixed = mixed_ref[...]
    mixedt_ref[...] = turned(mixed)
    n1, r1 = norm_stats(x.astype(F32) + mm(mixed, wout[...]) + bias[2:3])
    first = (n1 * gain[0:1] + bias[3:4]).astype(BF16)
    firstt_ref[...] = turned(first)
    copies[2].wait()
    copies[3].wait()
    total = first.astype(F32) + bias[4:5]
    chunks = [slice(c * ff_chunk, (c + 1) * ff_chunk) for c in range(inners // ff_chunk)]
    inner = [mm(first, wup[:, cols]) for cols in chunks]
    for c, cols in enumerate(chunks):
        hidden, slope = gelu_both(inner[c] + up_bias[:, cols])
        hidden = hidden.astype(BF16)
        hiddent_ref[cols, :] = turned(hidden)
        slope_ref[:, cols] = slope.astype(F32)
        total = total + mm(hidden, wdown[cols, :])
    n2, r2 = norm_stats(total)
    mine = pl.ds(pl.multiple_of(me * own, own), own)
    whole_ref[0] = (n2 * gain[1:2] + bias[5:6]).astype(BF16).astype(F32)
    ccls_ref[...] = whole_ref[0, mine, :]
    for i in (0, 5, 6, 7, 8):
        writes[i].start()

    def row_sum(values):
        return jnp.sum(values.astype(F32), axis=0, keepdims=True)

    sums_ref[0:1, :] = row_sum(gy * n2)
    sums_ref[1:2, :] = row_sum(gy)
    g_two = norm_back(gy, gain[1:2], n2, r2)
    g_second = g_two.astype(BF16)
    gsecond_ref[...] = g_second
    sums_ref[2:3, :] = row_sum(g_second)
    g_first = g_two
    g_hidden = [mm_nt(g_second, wdown[cols, :]) for cols in chunks]
    for c, cols in enumerate(chunks):
        g_inner = (g_hidden[c] * slope_ref[:, cols]).astype(BF16)
        ginner_ref[:, cols] = g_inner
        bsums_ref[:, cols] = row_sum(g_inner)
        g_first = g_first + mm_nt(g_inner, wup[:, cols])
    sums_ref[3:4, :] = row_sum(g_first * n1)
    sums_ref[4:5, :] = row_sum(g_first)
    g_one = norm_back(g_first, gain[0:1], n1, r1)
    g_branch = g_one.astype(BF16)
    gbranch_ref[...] = g_branch
    sums_ref[5:6, :] = row_sum(g_branch)
    for i in (10, 11, 12):
        writes[i].start()
    g_mixed = mm_nt(g_branch, wout[...]).astype(BF16)
    g_out = [stack_heads(g_mixed[:, at[0]]) for at in lanes]
    g_p = [mm_nt(qkv_ref[:, at[2]], g_out[pair]) for pair, at in enumerate(lanes)]
    g_s, g_st = [], []
    for pair in pairs:
        p = probs_ref[pair]
        g = p * (g_p[pair] - jnp.sum(g_p[pair] * p, axis=0, keepdims=True))
        g_s.append(g.astype(BF16))
        g_st.append(g.T.astype(BF16))
    for pair, at in enumerate(lanes):
        q, k, _ = (qkv_ref[:, part] for part in at)
        g_q = jnp.where(low, mm(g_st[pair][:rows], k), mm(g_st[pair][rows:], k)) * HDIM**-0.5
        gqkv_ref[:, at[0]] = g_q.astype(BF16)
        gqkv_ref[:, at[1]] = mm(g_s[pair], stack_heads(q * HDIM**-0.5)).astype(BF16)
        gqkv_ref[:, at[2]] = mm(probs_ref[pair].astype(BF16), g_out[pair]).astype(BF16)
    g_qkv = gqkv_ref[...]
    sums_ref[6:7, :] = row_sum(g_qkv[:, :width])
    sums_ref[7:8, :] = row_sum(g_qkv[:, 2 * width :])
    g_x = g_one + mm_nt(g_qkv, wqkv[...])
    whole_ref[1] = g_x
    gcls_ref[...] = whole_ref[1, mine, :]
    gpos_ref[...] = lax.dot_general(onehot, g_x, (((0,), (0,)), ((), ())), preferred_element_type=F32, precision=lax.Precision.HIGHEST)
    for i in (1, 2, 3, 4, 9):
        writes[i].start()
    for write in writes:
        write.wait()


def forward_kernel(
    x_ref, wqkv_hbm, wout_hbm, wup_hbm, wdown_hbm, cot_hbm, bias_ref, gain_ref, bup_ref, doc_ref, table_ref,
    qkv_ref, probs_ref, n1_ref, r1_ref, slope_ref, n2_ref, r2_ref, y_ref, xt_ref, mixedt_ref, firstt_ref, hiddent_ref,
    *refs, ff_chunk, devices,
):
    homes, outs, refs = refs[:OUTS], refs[OUTS : 2 * OUTS], refs[2 * OUTS :]
    wqkv, wout, wup, wdown, mixed_ref, first_ref, sems, cls_ref, cot_rows, cot_low, packed, gathered = refs[:12]
    cross_weights, cross_scratch = refs[12:16], refs[16:21]
    cross_sems, out_sems, cot_sems, send_sems, recv_sems = refs[21:]
    step = pl.program_id(0)
    last = pl.num_programs(0) - 1
    rows, width = x_ref.shape
    parts = [slice(part * width, (part + 1) * width) for part in range(3)]
    part_copies = [pltpu.make_async_copy(wqkv_hbm.at[0, :, cols], wqkv.at[:, cols], sems.at[3 + i]) for i, cols in enumerate(parts)]
    copies = part_copies + [
        pltpu.make_async_copy(src.at[0], dst, sems.at[i])
        for i, (src, dst) in enumerate(((wout_hbm, wout), (wup_hbm, wup), (wdown_hbm, wdown)))
    ]

    own = cls_ref.shape[0]
    line, me = lax.axis_index("row"), lax.axis_index("seg")
    peers = [(line, lax.rem(me + hop, devices)) for hop in range(1, devices)]
    cot_copies = [
        pltpu.make_async_copy(cot_hbm.at[pl.ds(i * SEGLEN, 16)], cot_rows.at[i], cot_sems.at[i]) for i in range(own)
    ]
    cross_copies = [
        pltpu.make_async_copy(src.at[1], dst, cross_sems.at[i])
        for i, (src, dst) in enumerate(zip((wqkv_hbm, wout_hbm, wup_hbm, wdown_hbm), cross_weights))
    ]
    writes = [pltpu.make_async_copy(src, dst, out_sems.at[i]) for i, (src, dst) in enumerate(zip(outs, homes))]
    barrier = pltpu.get_barrier_semaphore()

    def sends(kind):
        return [
            pltpu.make_async_remote_copy(
                src_ref=packed.at[kind], dst_ref=gathered.at[kind, hop + 1], send_sem=send_sems.at[kind, hop],
                recv_sem=recv_sems.at[kind, hop], device_id=peer, device_id_type=MESH,
            )
            for hop, peer in enumerate(peers)
        ]

    def arrived(kind, whole_ref):
        for send in sends(kind):
            send.wait()
        gathered[kind, 0] = packed[kind]
        for hop in range(devices):
            rows_at = pl.ds(pl.multiple_of(lax.rem(me - hop + devices, devices) * own, own), own)
            whole_ref[1 - kind, rows_at, :] = gathered[kind, hop].astype(F32)

    @pl.when(step == 0)
    def _():
        for peer in peers:
            pl.semaphore_signal(barrier, inc=1, device_id=peer, device_id_type=MESH)
        for copy in copies[:4]:
            copy.start()

    @pl.when(step == 1)
    def _():
        copies[4].wait()
        copies[5].wait()
        for copy in cot_copies + cross_copies:
            copy.start()

    @pl.when(step == 2)
    def _():
        for i, copy in enumerate(cot_copies):
            copy.wait()
            cot_low[i : i + 1, :] = cot_rows[i, 0:8, :].astype(F32)[0:1]
        packed[0] = cot_low[...].astype(BF16)
        pl.semaphore_wait(barrier, devices - 1)
        for send in sends(0):
            send.start()

    bias = bias_ref[...].astype(F32)[:, 0]
    gain = gain_ref[0].astype(F32)
    up_bias = bup_ref[0:1, :].astype(F32)
    inners = wup.shape[1]
    chunks = [slice(c * ff_chunk, (c + 1) * ff_chunk) for c in range(inners // ff_chunk)]
    items = [(seg, pair) for seg in range(rows // SEGLEN) for pair in range(width // LANES)]
    every = range(len(items))
    at = [slice(seg * SEGLEN, (seg + 1) * SEGLEN) for seg, _ in items]

    def front(state, loading):
        def project_part(part):
            if loading:
                copies[part].wait()
                if part == 0:
                    copies[4].start()
                    copies[5].start()
            x = x_ref[...]
            out = mm(x, wqkv[:, part * width : (part + 1) * width])
            if part == 0:
                out = out + bias[0:1]
            if part == 2:
                out = out + bias[1:2]
            out = out.astype(BF16)
            for group in range(width // GROUP):
                qkv_ref[group, :, part * GROUP : (part + 1) * GROUP] = out[:, group * GROUP : (group + 1) * GROUP]

        def piece(e, part):
            pair = items[e][1]
            return qkv_ref[pair // 2, at[e], pair_lanes(pair % 2)[part]]

        def scores():
            xt_ref[...] = x_ref[...].T
            state["scores"] = [mm_nt(piece(e, 1), stack_heads(piece(e, 0) * HDIM**-0.5)) for e in every]

        def softmax(part):
            for e in every[part :: 2]:
                score = state["scores"][e]
                ex = jnp.exp(score - jnp.max(score, axis=0, keepdims=True))
                p = (ex * (1.0 / jnp.sum(ex, axis=0, keepdims=True))).astype(BF16)
                probs_ref[items[e][0], items[e][1]] = p
                state[e] = jnp.concatenate([p[:, :SEGLEN].T, p[:, SEGLEN:].T], axis=1)

        def mix():
            for e, (_, pair) in enumerate(items):
                mixed_ref[at[e], pair * LANES : (pair + 1) * LANES] = mm(state[e], stack_heads(piece(e, 2))).astype(BF16)

        def project_out():
            if loading:
                copies[3].wait()
            mixed = mixed_ref[...]
            mixedt_ref[...] = mixed.T
            state["resid"] = x_ref[...].astype(F32) + mm(mixed, wout[...]) + bias[2:3]

        def norm():
            n1, r1 = norm_stats(state["resid"])
            n1_ref[...] = n1.astype(BF16)
            r1_ref[...] = jnp.broadcast_to(r1, r1_ref.shape)
            first = (n1 * gain[0:1] + bias[3:4]).astype(BF16)
            firstt_ref[...] = first.T
            state["first"] = first

        return [lambda part=part: project_part(part) for part in range(3)] + [scores, lambda: softmax(0), lambda: softmax(1), mix, project_out, norm]

    def back(state):
        first = first_ref[...]
        state["total"] = first.astype(F32) + bias[4:5]

        def up(c):
            state["inner", c] = mm(first, wup[:, chunks[c]])

        def gelu(c):
            cols = chunks[c]
            hidden, slope = gelu_both(state["inner", c] + up_bias[:, cols])
            hidden = hidden.astype(BF16)
            hiddent_ref[cols, :] = hidden.T
            slope_ref[:, cols] = slope.astype(BF16)
            state["hidden", c] = hidden

        def down(c):
            state["total"] = state["total"] + mm(state["hidden", c], wdown[chunks[c], :])

        def norm():
            n2, r2 = norm_stats(state["total"])
            n2_ref[...] = n2.astype(BF16)
            r2_ref[...] = jnp.broadcast_to(r2, r2_ref.shape)
            y = (n2 * gain[1:2] + bias[5:6]).astype(BF16)
            y_ref[...] = y
            segs = rows // SEGLEN
            for seg in range(segs):
                cls_ref[pl.ds((step - 1) * segs + seg, 1), :] = y[seg * SEGLEN : seg * SEGLEN + 8].astype(F32)[0:1]

        pieces = [lambda: up(0)]
        for c in range(len(chunks)):
            if c + 1 < len(chunks):
                pieces.append(lambda c=c: up(c + 1))
            pieces += [lambda c=c: gelu(c), lambda c=c: down(c)]
        return pieces + [norm]

    def run(with_front, with_back):
        state = {}
        lists = ([back(state)] if with_back else []) + ([front(state, not with_back)] if with_front else [])
        turns = sorted((((i + 0.5) / len(pieces), k, i) for k, pieces in enumerate(lists) for i in range(len(pieces))))
        for _, k, i in turns:
            lists[k][i]()
        if with_front:
            first_ref[...] = state["first"]

    @pl.when(step == 0)
    def _():
        run(True, False)

    @pl.when((step > 0) & (step < last))
    def _():
        run(True, True)

    @pl.when(step == last)
    def _():
        run(False, True)
        packed[1] = cls_ref[...].astype(BF16)
        for send in sends(1):
            send.start()
        arrived(0, cross_scratch[-1])
        arrived(1, cross_scratch[-1])
        cross_part(
            me, doc_ref, table_ref, bias_ref, gain_ref, bup_ref, outs, writes,
            cross_weights, cross_copies, cross_scratch, ff_chunk,
        )


def forward_blocks(x, cot, w_qkv, w_out, w_up, w_down, bias, gain, bup, docs, table, devices, tile=256, ff_chunk=768):
    total, width = x.shape
    inners = w_up.shape[-1]
    segs = tile // SEGLEN
    pairs = width // LANES
    any_spec = pl.BlockSpec(memory_space=pl.ANY)

    steps = total // tile

    def rows_of(cols, late):
        return pl.BlockSpec((tile, cols), lambda i: (jnp.maximum(i - 1, 0) if late else jnp.minimum(i, steps - 1), 0))

    def whole(a):
        return pl.BlockSpec(a.shape, lambda i: (0,) * a.ndim)

    def cols_of(rows, late):
        return pl.BlockSpec((rows, tile), lambda i: (0, jnp.maximum(i - 1, 0) if late else jnp.minimum(i, steps - 1)))

    outs = [
        ((width // GROUP, total, 3 * GROUP), BF16, pl.BlockSpec((width // GROUP, tile, 3 * GROUP), lambda i: (0, jnp.minimum(i, steps - 1), 0))),
        ((total // SEGLEN, pairs, SEGLEN, 2 * SEGLEN), BF16, pl.BlockSpec((segs, pairs, SEGLEN, 2 * SEGLEN), lambda i: (jnp.minimum(i, steps - 1), 0, 0, 0))),
        ((total, width), BF16, rows_of(width, False)),
        ((total, LANES), F32, rows_of(LANES, False)),
        ((total, inners), BF16, rows_of(inners, True)),
        ((total, width), BF16, rows_of(width, True)),
        ((total, LANES), F32, rows_of(LANES, True)),
        ((total, width), BF16, rows_of(width, True)),
        ((width, total), BF16, cols_of(width, False)),
        ((width, total), BF16, cols_of(width, False)),
        ((width, total), BF16, cols_of(width, False)),
        ((inners, total), BF16, cols_of(inners, True)),
    ]
    own = total // SEGLEN
    rows = own * devices
    cross_outs = [
        ((own, width), F32), ((own, width), F32), ((8, width), F32), ((1, inners), F32), (table.shape, F32),
        ((width, rows), BF16), ((width, rows), BF16), ((width, rows), BF16), ((inners, rows), BF16),
        ((rows, 3 * width), BF16), ((rows, width), BF16), ((rows, inners), BF16), ((rows, width), BF16),
    ]
    bias = bias.transpose(1, 0, 2)
    dma = pltpu.SemaphoreType.DMA
    return pl.pallas_call(
        functools.partial(forward_kernel, ff_chunk=ff_chunk, devices=devices),
        grid=(steps + 1,),
        in_specs=[rows_of(width, False), any_spec, any_spec, any_spec, any_spec, any_spec]
        + [whole(a) for a in (bias, gain, bup, docs, table)],
        out_specs=[o[2] for o in outs] + [pl.BlockSpec(memory_space=pltpu.HBM)] * OUTS,
        out_shape=[jax.ShapeDtypeStruct(o[0], o[1]) for o in outs + cross_outs],
        scratch_shapes=[pltpu.VMEM(*o) for o in cross_outs]
        + [
            pltpu.VMEM(w_qkv.shape[1:], BF16),
            pltpu.VMEM(w_out.shape[1:], BF16),
            pltpu.VMEM(w_up.shape[1:], BF16),
            pltpu.VMEM(w_down.shape[1:], BF16),
            pltpu.VMEM((tile, width), BF16),
            pltpu.VMEM((tile, width), BF16),
            dma((6,)),
            pltpu.VMEM((own, width), F32),
            pltpu.VMEM((own, 16, width), BF16),
            pltpu.VMEM((own, width), F32),
            pltpu.VMEM((2, own, width), BF16),
            pltpu.VMEM((2, devices, own, width), BF16),
            pltpu.VMEM(w_qkv.shape[1:], BF16),
            pltpu.VMEM(w_out.shape[1:], BF16),
            pltpu.VMEM(w_up.shape[1:], BF16),
            pltpu.VMEM(w_down.shape[1:], BF16),
            pltpu.VMEM((rows, 3 * width), BF16),
            pltpu.VMEM((pairs, rows, 2 * rows), F32),
            pltpu.VMEM((rows, width), BF16),
            pltpu.VMEM((rows, inners), F32),
            pltpu.VMEM((2, rows, width), F32),
            dma((4,)), dma((OUTS,)), dma((own,)), dma((2, devices - 1)), dma((2, devices - 1)),
        ],
        compiler_params=pltpu.CompilerParams(vmem_limit_bytes=63 * 2**20, collective_id=0, has_side_effects=True),
        name="forward_blocks",
    )(x, w_qkv, w_out, w_up, w_down, cot, bias, gain, bup, docs, table)

def fold_rows(values):
    rows, cols = values.shape
    return jnp.sum(values.reshape(rows // 8, 8, cols), axis=0)


def early_kernel(
    gcls_ref, ccls_ref, cot_ref, y_ref, n2_ref, r2_ref, slope_ref, n1_ref, r1_ref, wup_hbm, wdown_hbm, gain_ref,
    out_ref, gsecond_ref, ginner_ref, gbranch_ref, sums_ref, bsums_ref, wup, wdown, two_ref, sems, *, ff_chunk,
):
    step = pl.program_id(0)
    last = pl.num_programs(0) - 1
    copies = [
        pltpu.make_async_copy(src.at[0], dst, sems.at[i]) for i, (src, dst) in enumerate(((wdown_hbm, wdown), (wup_hbm, wup)))
    ]

    @pl.when(step == 0)
    def _():
        for copy in copies:
            copy.start()
        sums_ref[...] = jnp.zeros_like(sums_ref)
        bsums_ref[...] = jnp.zeros_like(bsums_ref)

    @pl.when(step == 1)
    def _():
        for copy in copies:
            copy.wait()

    rows, width = cot_ref.shape
    segs = rows // SEGLEN
    inners = wup.shape[1]
    gain = gain_ref[0].astype(F32)
    chunks = [slice(c * ff_chunk, (c + 1) * ff_chunk) for c in range(inners // ff_chunk)]

    def front(state):
        def gradient():
            place = lax.broadcasted_iota(jnp.int32, (rows, width), 0)
            gy = cot_ref[...].astype(F32)
            y = y_ref[...].astype(F32)
            for seg in range(segs):
                at = pl.ds(step * segs + seg, 1)
                gy = jnp.where(place == seg * SEGLEN, gcls_ref[at, :], gy)
                y = jnp.where(place == seg * SEGLEN, ccls_ref[at, :], y)
            out_ref[...] = y.astype(BF16)
            state["gy"] = gy

        def norm():
            gy = state["gy"]
            n2 = n2_ref[...].astype(F32)
            sums_ref[0] += fold_rows(gy * n2)
            sums_ref[1] += fold_rows(gy)
            state["two"] = norm_back(gy, gain[1:2], n2, r2_ref[:, 0:1])

        def store():
            low = state["two"].astype(BF16)
            gsecond_ref[...] = low
            sums_ref[2] += fold_rows(low.astype(F32))

        return [gradient, norm, store]

    def back(state):
        g_two = two_ref[...]
        g_second = g_two.astype(BF16)
        state["first"] = g_two

        def down(c):
            state["hidden", c] = mm_nt(g_second, wdown[chunks[c], :])

        def slope(c):
            cols = chunks[c]
            g_low = state["hidden", c].astype(BF16) * slope_ref[:, cols]
            ginner_ref[:, cols] = g_low
            bsums_ref[:, cols] += fold_rows(g_low.astype(F32))
            state["inner", c] = g_low

        def up(c):
            state["first"] = state["first"] + mm_nt(state["inner", c], wup[:, chunks[c]])

        def norm():
            g_first = state["first"]
            n1 = n1_ref[...].astype(F32)
            sums_ref[3] += fold_rows(g_first * n1)
            sums_ref[4] += fold_rows(g_first)
            g_branch = norm_back(g_first, gain[0:1], n1, r1_ref[:, 0:1]).astype(BF16)
            gbranch_ref[...] = g_branch
            sums_ref[5] += fold_rows(g_branch.astype(F32))

        pieces = [lambda: down(0)]
        for c in range(len(chunks)):
            if c + 1 < len(chunks):
                pieces.append(lambda c=c: down(c + 1))
            pieces += [lambda c=c: slope(c), lambda c=c: up(c)]
        return pieces + [norm]

    def run(with_front, with_back):
        state = {}
        lists = ([back(state)] if with_back else []) + ([front(state)] if with_front else [])
        turns = sorted((((i + 0.5) / len(pieces), k, i) for k, pieces in enumerate(lists) for i in range(len(pieces))))
        for _, k, i in turns:
            lists[k][i]()
        if with_front:
            two_ref[...] = state["two"]

    @pl.when(step == 0)
    def _():
        run(True, False)

    @pl.when((step > 0) & (step < last))
    def _():
        run(True, True)

    @pl.when(step == last)
    def _():
        run(False, True)


def early_backward(gcls, ccls, cot, y, n2, r2, slope, n1, r1, w_up, w_down, gains, tile=256, ff_chunk=768):
    total, width = cot.shape
    inners = w_up.shape[-1]
    any_spec = pl.BlockSpec(memory_space=pl.ANY)

    steps = total // tile

    def rows_of(cols, late=False):
        return pl.BlockSpec((tile, cols), lambda i: (jnp.maximum(i - 1, 0) if late else jnp.minimum(i, steps - 1), 0))

    def whole(a):
        return pl.BlockSpec(a.shape, lambda i: (0,) * len(a.shape))

    outs = [
        ((total, width), BF16, rows_of(width)),
        ((total, width), BF16, rows_of(width)),
        ((total, inners), BF16, rows_of(inners, True)),
        ((total, width), BF16, rows_of(width, True)),
        ((6, 8, width), F32, pl.BlockSpec((6, 8, width), lambda i: (0, 0, 0))),
        ((8, inners), F32, pl.BlockSpec((8, inners), lambda i: (0, 0))),
    ]
    return pl.pallas_call(
        functools.partial(early_kernel, ff_chunk=ff_chunk),
        grid=(steps + 1,),
        in_specs=[whole(gcls), whole(ccls), rows_of(width), rows_of(width), rows_of(width), rows_of(LANES), rows_of(inners, True),
                  rows_of(width, True), rows_of(LANES, True), any_spec, any_spec, whole(gains)],
        out_specs=[o[2] for o in outs],
        out_shape=[jax.ShapeDtypeStruct(o[0], o[1]) for o in outs],
        scratch_shapes=[pltpu.VMEM(w_up.shape[1:], BF16), pltpu.VMEM(w_down.shape[1:], BF16), pltpu.VMEM((tile, width), F32), pltpu.SemaphoreType.DMA((2,))],
        compiler_params=pltpu.CompilerParams(vmem_limit_bytes=60 * 2**20),
        name="early_backward",
    )(gcls, ccls, cot, y, n2, r2, slope, n1, r1, w_up, w_down, gains)

RING = 4
CROSS_UNITS = 3
SEG_UNITS = 12
UNITS = CROSS_UNITS + SEG_UNITS
CHAINS = UNITS + 1
PART = 48
GROUPS = 3
EARLY = 9
TILES = 4
GROUP_STEPS = TILES + 1
LAST_AT = EARLY + GROUPS * GROUP_STEPS
STEPS = LAST_AT + TILES


CHAIN_TABLE = (
    ("e", 1, 4, 6, 8, 13), ("a", 1, 4, 6, 8, 13), ("e", 2, 6, 8, 11, 16), ("a", 2, 6, 8, 11, 16),
    ("e", 4, 8, 11, 14, 19), ("a", 4, 8, 11, 14, 19), ("b", 6, 11, 14, 17, 21), ("a", 6, 11, 14, 17, 21),
    ("b", 8, 14, 17, 20, 24), ("a", 8, 14, 17, 20, 24), ("b", 11, 17, 20, 23, 26), ("a", 11, 17, 20, 23, 26),
    ("b", 14, 18, 21, 23, 26), ("a", 19, 23, 25, 27, 28), ("b", 24, 26, 27, 28, 28), ("a", 24, 26, 27, 28, 28),
)
SMALL_MOMENTS = (1, 4, 6, 8, 10, 12)
SMALL_LATE = (23, 24, 25, 26, 27, 28)
WAYS = "".join(row[0] for row in CHAIN_TABLE)


def comm_schedule():
    table = {s: [] for s in range(STEPS + 1)}
    for n, (_, *moments) in enumerate(CHAIN_TABLE):
        for action, at in zip(("send", "two", "three", "final", "out"), moments):
            if action != "send" or n not in (1, 3):
                table[at].append((action, n))
    for n, at in ((CROSS_UNITS + EARLY - 1, EARLY + 1), (UNITS - 3, 14), (UNITS - 2, 19), (UNITS - 1, 24)):
        table[at].append(("one", n))
    for d in range(6):
        table[SMALL_MOMENTS[d]].append(("small", d))
        table[SMALL_LATE[d]].append(("late", d))
    order = ("small", "late", "one", "out", "final", "three", "two", "send")
    for at in range(STEPS):
        table[at].sort(key=lambda item: (order.index(item[0]), item[1]))
    rank = {"two": 1, "three": 2, "final": 3, "out": 4}
    table[STEPS].sort(key=lambda item: (rank[item[0]] if item[0] != "late" else item[1] - 2.5, item[1]))
    return table


def add_low(a, b):
    return (a.astype(F32) + b.astype(F32)).astype(BF16)


def late_kernel(
    firstt, ginner, hiddent, gsecond, mixedt, gbranch, xt, qkv, probs, wqkv_hbm, wout_hbm,
    cfirstt, cginner, chiddent, cgsecond, cmixedt, cgbranch, cxt, cgqkv,
    sums, bsums, csums, cbsums, gpos,
    dqkv_ref, dout_ref, dup_ref, ddown_ref, small_ref, gx_ref,
    aslot, bslot, qkv_slot, probs_slot, gbranch_slot, gx_slot, wqkv, wout, fold, csend, crecv, keep, r1, r2, r3, rf, rc, acc, racc, late_acc, late_racc,
    load_sems, tile_sems, store_sems, weight_sems, csend_sems, crecv_sems, s1_sems, q1_sems, s2_sems, q2_sems, s3_sems, q3_sems, sf_sems, qf_sems, sa_sems, qa_sems,
    *, share,
):
    width = bslot.shape[-1]
    line, z = lax.axis_index("row"), lax.axis_index("seg")
    y, x, c = line // 4, (line // 2) % 2, line % 2
    zh, zl = z // 2, z % 2
    flip_c = (y * 4 + x * 2 + 1 - c, z)
    flip_x = (y * 4 + (1 - x) * 2 + c, z)
    flip_y = ((1 - y) * 4 + x * 2 + c, z)
    flip_zl = (line, zh * 2 + 1 - zl)
    flip_zh = (line, (1 - zh) * 2 + zl)
    flip_yzh = ((1 - y) * 4 + x * 2 + c, (1 - zh) * 2 + zl)
    barrier = pltpu.get_barrier_semaphore()
    for peer in (flip_c, flip_x, flip_y, flip_zl, flip_zh, flip_yzh):
        pl.semaphore_signal(barrier, inc=1, device_id=peer, device_id_type=MESH)

    tile = gbranch_slot.shape[1]
    segs = tile // SEGLEN

    def a_slot(u):
        return jnp.where((u < 4) | (u >= EARLY), 0, (u + 1) % 2)

    def b_slot(u):
        return jnp.where(u < 4, u % 2, jnp.where(u < EARLY, u // 8, u - EARLY))

    def load_unit(u, do):
        def act(src, dst, side):
            getattr(pltpu.make_async_copy(src, dst, load_sems.at[side]), do)()

        def columns(ref, j):
            return ref.at[:, pl.ds(pl.multiple_of(j * width, width), width)]

        @pl.when(u == 0)
        def _():
            act(firstt, aslot.at[0], 0)

        @pl.when(u < 4)
        def _():
            act(columns(ginner, u), bslot.at[u % 2], 1)

        @pl.when((u >= 4) & (u < 8))
        def _():
            act(hiddent.at[:, :, :, u - 4], aslot.at[(u + 1) % 2], 0)

        @pl.when(u == 4)
        def _():
            act(gsecond, bslot.at[0], 1)

        @pl.when(u == 8)
        def _():
            act(mixedt, aslot.at[1], 0)
            act(gbranch, bslot.at[1], 1)

        @pl.when(u == EARLY)
        def _():
            act(xt, aslot.at[0], 0)

    def tile_rows(i):
        return pl.ds(pl.multiple_of(i * tile, tile), tile)

    def load_tile(j, i, slot, late, do):
        copies = [pltpu.make_async_copy(gbranch.at[tile_rows(i)], gbranch_slot.at[slot], tile_sems.at[slot, 0])]
        if not late:
            copies.append(pltpu.make_async_copy(qkv.at[j, tile_rows(i)], qkv_slot.at[slot], tile_sems.at[slot, 1]))
            copies.append(
                pltpu.make_async_copy(probs.at[pl.ds(i * segs, segs), pl.ds(2 * j, 2)], probs_slot.at[slot], tile_sems.at[slot, 2])
            )
        for copy in copies:
            getattr(copy, do)()

    def place(s):
        group = (s - EARLY) // GROUP_STEPS
        return group, (s - EARLY) % GROUP_STEPS

    def load(s, do):
        group, part = place(s)
        inside = (s >= EARLY) & (s < LAST_AT)

        @pl.when(s < EARLY)
        def _():
            load_unit(s, do)

        @pl.when(inside & (part < TILES))
        def _():
            load_tile(group, part, part % 2, False, do)

        @pl.when(inside & (part == TILES))
        def _():
            load_unit(EARLY + group, do)

        @pl.when(s >= LAST_AT)
        def _():
            load_tile(0, s - LAST_AT, (s - LAST_AT) % 2, True, do)

    def store_gx(i):
        return pltpu.make_async_copy(gx_slot.at[i % 2], gx_ref.at[tile_rows(i)], store_sems.at[i % 2])

    weight_copies = [pltpu.make_async_copy(wout_hbm.at[0], wout, weight_sems.at[0])]
    for j in range(GROUPS):
        for part in range(3):
            weight_copies.append(
                pltpu.make_async_copy(
                    wqkv_hbm.at[0, :, pl.ds(part * width + j * GROUP, GROUP)],
                    wqkv.at[j, :, pl.ds(part * GROUP, GROUP)],
                    weight_sems.at[1 + 3 * j + part],
                )
            )
    load(0, "start")

    def remote(src, dst, send_sem, recv_sem, peer):
        return pltpu.make_async_remote_copy(
            src_ref=src, dst_ref=dst, send_sem=send_sem, recv_sem=recv_sem, device_id=peer, device_id_type=MESH
        )

    ways = {
        "a": ((x, zl, zh), (flip_x, flip_zl, flip_zh)),
        "b": ((y, x, zl), (flip_y, flip_x, flip_zl)),
        "c": ((zl, x, zh), (flip_zl, flip_x, flip_zh)),
        "e": ((y, x), (flip_y, flip_x)),
        "f": ((x,), (flip_x,)),
    }

    def way(n):
        return ways[WAYS[n]]

    def among(n, kinds, chains):
        return sum((jnp.asarray(n == k).astype(jnp.int32) for k in chains if WAYS[k] in kinds), jnp.int32(0))

    def block_place(in_b, in_c, far, high, low):
        at = {"a": far * 4 + low * 2 + high, "b": high * 4 + far * 2 + low, "c": low * 4 + far * 2 + high}
        return at["a"] + in_b * (at["b"] - at["a"]) + in_c * (at["c"] - at["a"])

    def core_copy(n):
        slot = n % RING
        return remote(csend.at[slot], crecv.at[slot], csend_sems.at[slot], crecv_sems.at[slot], flip_c)

    def part_of(n):
        if n >= UNITS - 1:
            half = width // 2
            return UNITS - 1, slice((n - UNITS + 1) * half, (n - UNITS + 2) * half)
        return n, slice(0, width)

    def copy_one(n):
        (b1, *_), (peer, *_) = way(n)
        m, cols = part_of(n)
        return remote(keep.at[m, pl.ds(4 * (1 - b1), 4), :, cols], r1.at[m, :, :, cols], s1_sems.at[n], q1_sems.at[n], peer)

    def copy_two(n):
        (b1, b2, *_), (_, peer, *_) = way(n)
        m, cols = part_of(n)
        return remote(keep.at[m, pl.ds(4 * b1 + 2 * (1 - b2), 2), :, cols], r2.at[m, :, :, cols], s2_sems.at[n], q2_sems.at[n], peer)

    def copy_three(n):
        (b1, b2, b3), (_, _, peer) = way(n)
        m, cols = part_of(n)
        return remote(keep.at[m, 4 * b1 + 2 * b2 + 1 - b3, :, cols], r3.at[m, :, cols], s3_sems.at[n], q3_sems.at[n], peer)

    def own_block(n):
        (b1, b2, b3), _ = way(n)
        m, cols = part_of(n)
        return keep.at[m, 4 * b1 + 2 * b2 + b3, :, cols]

    def step_one(n):
        core_copy(n).wait_recv()
        keep[n] = add_low(keep[n], crecv[n % RING])

    def step_two(n):
        (b1, *_), _ = way(n)
        copy_one(n).wait()
        m, cols = part_of(n)
        at = pl.ds(4 * b1, 4)
        keep[m, at, :, cols] = add_low(keep[m, at, :, cols], r1[m, :, :, cols])
        if WAYS[n] != "f":
            copy_two(n).start()

    def step_three(n):
        if WAYS[n] == "f":
            return
        (b1, b2, *_), _ = way(n)
        copy_two(n).wait()
        m, cols = part_of(n)
        at = pl.ds(4 * b1 + 2 * b2, 2)
        keep[m, at, :, cols] = add_low(keep[m, at, :, cols], r2[m, :, :, cols])
        if WAYS[n] != "e":
            copy_three(n).start()

    def final_to(n, slot, peer):
        m, cols = part_of(n)
        return remote(own_block(n), rf.at[m, slot, :, cols], sf_sems.at[n], qf_sems.at[n, slot], peer)

    def sends_final(n, act):
        if WAYS[n] != "b":
            @pl.when(y == 1)
            def _():
                act(final_to(n, 0, flip_y))
            return

        @pl.when((y == 1) & (zh == 1))
        def _():
            act(final_to(n, 0, flip_y))

        @pl.when((y == 0) & (zh == 1))
        def _():
            act(final_to(n, 0, flip_zh))

        @pl.when((y == 1) & (zh == 0))
        def _():
            act(final_to(n, 1, flip_yzh))

    def cross_final(n):
        src = keep.at[n, pl.ds(2 * x, 2)] if WAYS[n] == "e" else keep.at[n, pl.ds(4 * x, 4)]
        count = 2 if WAYS[n] == "e" else 4
        return remote(src, rc.at[n // 2, pl.ds(0, count)], sf_sems.at[n], qf_sems.at[n, 0], flip_y)

    def step_final(n):
        if WAYS[n] in "ef":
            @pl.when(y == 0)
            def _():
                cross_final(n).start()
            return
        copy_three(n).wait()
        (b1, b2, b3), _ = way(n)
        m, cols = part_of(n)
        at = 4 * b1 + 2 * b2 + b3
        keep[m, at, :, cols] = add_low(keep[m, at, :, cols], r3[m, :, cols])
        sends_final(n, lambda copy: copy.start())

    def put(u, value, cols=slice(0, 16 * PART)):
        def columns(j):
            return pl.ds(pl.multiple_of(j * width, width), width)

        @pl.when(u < 4)
        def _():
            dup_ref[:, columns(u)] = value

        @pl.when((u >= 4) & (u < 8))
        def _():
            ddown_ref[pl.ds(pl.multiple_of((u - 4) * PART, PART), PART), :] = value

        @pl.when(u == 8)
        def _():
            dout_ref[...] = value

        for j in range(GROUPS):
            @pl.when(u == EARLY + j)
            def _(j=j):
                for part in range(3):
                    first, last = max(part * GROUP, cols.start), min((part + 1) * GROUP, cols.stop)
                    if first < last:
                        to = part * (width - GROUP) + j * GROUP
                        dqkv_ref[:, to + first : to + last] = value[:, first - cols.start : last - cols.start]

    def step_out(n):
        if WAYS[n] in "ef":
            return cross_step_out(n)
        m, cols = part_of(n)
        u = n // 2 if n < 2 * CROSS_UNITS else m - CROSS_UNITS
        sends_final(n, lambda copy: copy.wait_send())

        @pl.when(y == 0)
        def _():
            final_to(n, 0, flip_y).wait_recv()
            straight = (zh == 0) if WAYS[n] == "b" else (y == 0)

            @pl.when(straight)
            def _():
                put(u, own_block(n)[...].astype(F32) + rf[m, 0, :, cols].astype(F32), cols)

            if WAYS[n] == "b":
                @pl.when(zh == 1)
                def _():
                    final_to(n, 1, flip_y).wait_recv()
                    put(u, rf[m, 0, :, cols].astype(F32) + rf[m, 1, :, cols].astype(F32), cols)

    def cross_step_out(n):
        @pl.when(y == 0)
        def _():
            cross_final(n).wait_send()

        @pl.when(y == 1)
        def _():
            cross_final(n).wait_recv()
            for sub in range(4):
                if WAYS[n] == "f":
                    block = keep[n, 4 * x + sub].astype(F32) + rc[n // 2, sub].astype(F32)
                else:
                    block = (rc[n // 2, sub] if sub < 2 else keep[n, 4 + 2 * x + sub - 2]).astype(F32)
                put(2 * n + sub, block)

    small_peers = (flip_c, flip_x, flip_y, flip_zl, flip_zh)

    rounds = ((acc, racc), (late_acc, late_racc))

    def small_copy(late, d):
        own, other = rounds[late]
        return remote(own.at[d], other.at[d], sa_sems.at[late, d], qa_sems.at[late, d], small_peers[d])

    def small_step(late, d):
        own, other = rounds[late]
        small_copy(late, d).wait()
        own[d + 1] = own[d] + other[d]
        if d + 1 < len(small_peers):
            small_copy(late, d + 1).start()
        elif late:
            small_ref[0:8, :] = acc[d + 1, 0:8, :] + own[d + 1]
            small_ref[8:32, :] = acc[d + 1, 8:32, :]

    seg_rows = [jnp.sum(sums[i], axis=0, keepdims=True) for i in range(6)]
    seg_up = jnp.sum(bsums[...], axis=0, keepdims=True)
    order = (6, 7, 5, 4, 2, 1)
    for i, row in enumerate(order):
        if row < 6:
            acc[0, i : i + 1, :] = seg_rows[row]
        acc[0, 6 + i : 7 + i, :] = csums[row : row + 1, :] * share
    for i, row in enumerate((3, 0)):
        acc[0, 12 + i : 13 + i, :] = seg_rows[row]
        acc[0, 14 + i : 15 + i, :] = csums[row : row + 1, :] * share
    for i in range(4):
        acc[0, 16 + i : 17 + i, :] = seg_up[:, i * width : (i + 1) * width]
        acc[0, 20 + i : 21 + i, :] = cbsums[:, i * width : (i + 1) * width] * share
    acc[0, 0:2, :] = jnp.zeros_like(acc[0, 0:2, :])
    acc[0, 24:32, :] = gpos[...] * share
    late_acc[0] = jnp.zeros_like(late_acc[0])

    def cross_unit(n, parts):
        if n >= RING:
            core_copy(n).wait_send()
        for rel in (1, 0):
            core = c if rel == 0 else 1 - c
            for sub, (left, right) in enumerate(parts):
                for far in range(2):
                    value = mm(left(far, core), right).astype(BF16)
                    at = (sub // 2) * 4 + far * 2 + sub % 2 if WAYS[n] == "e" else far * 4 + sub
                    if rel == 1:
                        csend[n % RING, at] = value
                    else:
                        keep[n, at] = value
            if rel == 1:
                if n == 0:
                    pl.semaphore_wait(barrier, 6)
                core_copy(n).start()

    def plain(ref):
        return lambda far, core: ref[far, core, z]

    def nested(ref, j):
        return lambda far, core: ref[far, core, z, j]

    def cut(ref, j):
        return ref[:, j * width : (j + 1) * width]

    def cut_group(ref, j):
        return jnp.concatenate([ref[:, part * width + j * GROUP : part * width + (j + 1) * GROUP] for part in range(3)], axis=1)

    cross_parts = (
        lambda: [(plain(cfirstt), cut(cginner, j)) for j in range(4)],
        lambda: [(nested(chiddent, j), cgsecond[...]) for j in range(4)],
        lambda: [(plain(cmixedt), cgbranch[...])] + [(plain(cxt), cut_group(cgqkv, j)) for j in range(GROUPS)],
    )

    def compute(u):
        n = u + CROSS_UNITS - jnp.maximum(CROSS_UNITS - 1 - u, 0)
        @pl.when(n >= RING)
        def _():
            core_copy(n).wait_send()

        sides = []
        for side in range(2):
            chains, chain = tuple(range(UNITS - 1)) + (UNITS - 1 + side,), n + side * (n // (UNITS - 1))
            sides.append((among(chain, "b", chains), among(chain, "c", chains)))
        right = bslot[b_slot(u)]
        for rel in (1, 0):
            core = c if rel == 0 else 1 - c
            left = aslot[a_slot(u), :, core].reshape(8 * PART, -1)
            value = mm(left, right).astype(BF16)
            for far in range(2):
                for part in range(4):
                    block = value[(far * 4 + part) * PART : (far * 4 + part + 1) * PART]
                    for side in range(2):
                        at = block_place(*sides[side], far, part // 2, part % 2)
                        cols = slice(side * width // 2, (side + 1) * width // 2)
                        if rel == 1:
                            csend[n % RING, at, :, cols] = block[:, cols]
                        else:
                            keep[n, at, :, cols] = block[:, cols]
            if rel == 1:
                core_copy(n).start()

        @pl.when(n < CROSS_UNITS + EARLY)
        def _():
            step_one(n - 1)

    def attention_tile(j, i):
        slot = i % 2
        out_rows = pl.ds(pl.multiple_of(j * GROUP, GROUP), GROUP)
        g_mixed = mm_nt(gbranch_slot[slot], wout[out_rows, :]).astype(BF16)
        items = [(seg, half) for seg in range(segs) for half in range(2)]
        at = [slice(seg * SEGLEN, (seg + 1) * SEGLEN) for seg, _ in items]
        lanes = [pair_lanes(half) for _, half in items]
        to = [pl.ds(pl.multiple_of(i * tile + seg * SEGLEN, SEGLEN), SEGLEN) for seg, _ in items]
        every = range(len(items))
        g_out = [stack_heads(g_mixed[at[e], lanes[e][0]]) for e in every]
        g_p = [mm_nt(qkv_slot[slot, at[e], lanes[e][2]], g_out[e]) for e in every]
        g_v = [mm(probs_slot[slot, seg, half], g_out[e]) for e, (seg, half) in enumerate(items)]
        g_s = []
        for e, (seg, half) in enumerate(items):
            p = probs_slot[slot, seg, half].astype(F32)
            g_s.append((p * (g_p[e] - jnp.sum(g_p[e] * p, axis=0, keepdims=True))).astype(BF16))
        g_k = [mm(g_s[e], stack_heads(qkv_slot[slot, at[e], lanes[e][0]] * HDIM**-0.5)) for e in every]
        g_st = [jnp.concatenate([g_s[e][:, :SEGLEN].T, g_s[e][:, SEGLEN:].T], axis=1) for e in every]
        g_q = [mm(g_st[e], stack_heads(qkv_slot[slot, at[e], lanes[e][1]])) * HDIM**-0.5 for e in every]
        for e in every:
            for part, value in enumerate((g_q[e], g_k[e], g_v[e])):
                value = value.astype(BF16)
                bslot[j, to[e], lanes[e][part]] = value
                if part != 1:
                    fold[part // 2, j, :, lanes[e][0]] += fold_rows(value.astype(F32))

    def last_tile(i):
        slot = i % 2

        @pl.when(i >= 2)
        def _():
            store_gx(i - 2).wait()

        total = gbranch_slot[slot].astype(F32)
        for j in range(GROUPS):
            total = total + mm_nt(bslot[j, tile_rows(i), :], wqkv[j])
        gx_slot[slot] = total.astype(BF16)
        store_gx(i).start()

    def run(action, n):
        if action in ("small", "late"):
            late = int(action == "late")
            if late and n == 0:
                for row in range(2):
                    for j in range(GROUPS):
                        late_acc[0, row : row + 1, j * GROUP : (j + 1) * GROUP] = jnp.sum(fold[row, j], axis=0, keepdims=True)
            if n == 0:
                small_copy(late, 0).start()
            else:
                small_step(late, n - 1)
            return
        {
            "one": step_one, "send": lambda n: copy_one(n).start(), "two": step_two, "three": step_three, "final": step_final, "out": step_out,
        }[action](n)

    schedule = comm_schedule()

    def step(s, carry):
        for at in range(STEPS):
            if schedule[at]:
                @pl.when(s == at)
                def _(at=at):
                    for action, n in schedule[at]:
                        run(action, n)

        @pl.when(s == EARLY)
        def _():
            for copy in weight_copies:
                copy.wait()

        for i in range(1, CROSS_UNITS):
            @pl.when(s == i)
            def _(i=i):
                cross_unit(2 * i, cross_parts[i]())
                step_one(2 * i - 1)
                copy_one(2 * i - 1).start()

        load(s, "wait")

        @pl.when(s == 1)
        def _():
            for copy in weight_copies:
                copy.start()

        @pl.when(s + 1 < STEPS)
        def _():
            load(s + 1, "start")

        group, part = place(s)
        inside = (s >= EARLY) & (s < LAST_AT)
        multiply = (s < EARLY) | (inside & (part == TILES))

        @pl.when(multiply)
        def _():
            compute(jnp.where(s < EARLY, s, EARLY + group))

        @pl.when(inside & (part < TILES))
        def _():
            attention_tile(group, part)

        @pl.when(s >= LAST_AT)
        def _():
            last_tile(s - LAST_AT)

        return carry

    fold[...] = jnp.zeros_like(fold)
    cross_unit(0, cross_parts[0]())
    lax.fori_loop(0, STEPS, step, 0)
    for action, n in schedule[STEPS]:
        run(action, n)
    for i in range(TILES - 2, TILES):
        store_gx(i).wait()
    for n in range(UNITS - RING, UNITS):
        core_copy(n).wait_send()


def late_backward(big, cross, small, attn, share):
    firstt, ginner, hiddent, gsecond, mixedt, gbranch, xt = big
    qkv, probs, w_qkv, w_out = attn
    cfirstt, cginner, chiddent, cgsecond, cmixedt, cgbranch, cxt, cgqkv = cross
    width, depth = firstt.shape
    inners = ginner.shape[1]
    rows = cfirstt.shape[1]
    tile = depth // TILES
    assert width == 16 * PART and inners == 4 * width

    def blocks(a, n):
        return a.reshape((2, 2, 4) + ((n,) if n > 1 else ()) + (PART, a.shape[1]))

    operands = [
        blocks(firstt, 1), ginner, blocks(hiddent, 4), gsecond, blocks(mixedt, 1), gbranch, blocks(xt, 1), qkv, probs, w_qkv, w_out,
        blocks(cfirstt, 1), cginner, blocks(chiddent, 4), cgsecond, blocks(cmixedt, 1), cgbranch, blocks(cxt, 1), cgqkv, *small,
    ]
    vmem = pl.BlockSpec(memory_space=pltpu.VMEM)
    any_spec = pl.BlockSpec(memory_space=pl.ANY)
    outs = [((PART, 3 * width), F32), ((PART, width), F32), ((PART, inners), F32), ((4 * PART, width), F32), ((32, width), F32), ((depth, width), BF16)]
    segs = tile // SEGLEN
    dma = pltpu.SemaphoreType.DMA
    return pl.pallas_call(
        functools.partial(late_kernel, share=share),
        in_specs=[any_spec] * 11 + [vmem] * (len(operands) - 11),
        out_specs=[vmem] * 5 + [any_spec],
        out_shape=[jax.ShapeDtypeStruct(*o) for o in outs],
        scratch_shapes=[
            pltpu.VMEM((2, 2, 2, 4, PART, depth), BF16),
            pltpu.VMEM((GROUPS, depth, width), BF16),
            pltpu.VMEM((2, tile, width), BF16),
            pltpu.VMEM((2, segs, 2, SEGLEN, 2 * SEGLEN), BF16),
            pltpu.VMEM((2, tile, width), BF16),
            pltpu.VMEM((2, tile, width), BF16),
            pltpu.VMEM((GROUPS, width, 3 * GROUP), BF16),
            pltpu.VMEM(w_out.shape[1:], BF16),
            pltpu.VMEM((2, GROUPS, 8, GROUP), F32),
            pltpu.VMEM((RING, 8, PART, width), BF16),
            pltpu.VMEM((RING, 8, PART, width), BF16),
            pltpu.VMEM((UNITS, 8, PART, width), BF16),
            pltpu.VMEM((UNITS, 4, PART, width), BF16),
            pltpu.VMEM((UNITS, 2, PART, width), BF16),
            pltpu.VMEM((UNITS, PART, width), BF16),
            pltpu.VMEM((UNITS, 2, PART, width), BF16),
            pltpu.VMEM((CROSS_UNITS, 4, PART, width), BF16),
            pltpu.VMEM((6, 32, width), F32),
            pltpu.VMEM((5, 32, width), F32),
            pltpu.VMEM((6, 8, width), F32),
            pltpu.VMEM((5, 8, width), F32),
            dma((2,)), dma((2, 3)), dma((2,)), dma((1 + 3 * GROUPS,)), dma((RING,)), dma((RING,)), dma((CHAINS,)), dma((CHAINS,)), dma((CHAINS,)), dma((CHAINS,)),
            dma((CHAINS,)), dma((CHAINS,)), dma((CHAINS,)), dma((CHAINS, 2)), dma((2, 5)), dma((2, 5)),
        ],
        compiler_params=pltpu.CompilerParams(vmem_limit_bytes=63 * 2**20, collective_id=1, has_side_effects=True),
        name="late_backward",
    )(*operands)

def finish_kernel(gx_ref, a_ref, b_ref, c_ref, d_ref, gx_out, a_out, b_out, c_out, d_out):
    gx_out[...] = gx_ref[...].astype(F32)

    @pl.when(pl.program_id(0) == 0)
    def _():
        for src, dst in ((a_ref, a_out), (b_ref, b_out), (c_ref, c_out), (d_ref, d_out)):
            dst[...] = src[...]


def finish(gx, grads, tile=1024):
    total, width = gx.shape
    rows = pl.BlockSpec((tile, width), lambda i: (i, 0))
    held = [pl.BlockSpec(g.shape, lambda i: (0, 0)) for g in grads]
    return pl.pallas_call(
        finish_kernel,
        grid=(total // tile,),
        in_specs=[rows] + held,
        out_specs=[rows] + held,
        out_shape=[jax.ShapeDtypeStruct(gx.shape, F32)] + [jax.ShapeDtypeStruct(g.shape, F32) for g in grads],
        name="finish",
    )(gx, *grads)


def small_grads(sums, bsums, csums, cbsums, gpos, bias_sums, cross_share):
    seg_rows = jnp.concatenate([jnp.sum(sums, axis=1), bias_sums])
    cross_rows = csums * cross_share
    order = jnp.array([6, 7, 5, 4, 2, 1])
    biases = jnp.stack([seg_rows[order], cross_rows[order]])
    gains = jnp.stack([seg_rows[jnp.array([3, 0])], cross_rows[jnp.array([3, 0])]])
    ups = jnp.stack([jnp.sum(bsums, axis=0), cbsums[0] * cross_share])
    return biases.reshape(-1), gains.reshape(-1), ups.reshape(-1), (gpos * cross_share).reshape(-1)


def attention_back(qkv, probs, gbranch, w_qkv, w_out):
    total, width = gbranch.shape
    heads = width // HDIM
    segs = total // SEGLEN
    scale = HDIM**-0.5

    def split(a):
        return a.reshape(segs, SEGLEN, heads, HDIM)

    def merge(a):
        return a.reshape(total, width)

    q, k, v = (
        split(qkv[:, :, part * GROUP : (part + 1) * GROUP].transpose(1, 0, 2).reshape(total, width)) for part in range(3)
    )
    p_low = probs.reshape(segs, heads // 2, SEGLEN, 2, SEGLEN).transpose(0, 1, 3, 2, 4).reshape(segs, heads, SEGLEN, SEGLEN)
    g_out = split(mm_nt(gbranch, w_out).astype(BF16))
    p = p_low.astype(F32)
    g_p = jnp.einsum("sqhd,skhd->shkq", g_out, v, preferred_element_type=F32)
    g_s = (p * (g_p - jnp.sum(g_p * p, axis=2, keepdims=True))).astype(BF16)
    g_v = jnp.einsum("shkq,sqhd->skhd", p_low, g_out, preferred_element_type=F32)
    g_k = jnp.einsum("shkq,sqhd->skhd", g_s, q, preferred_element_type=F32) * scale
    g_q = jnp.einsum("shkq,skhd->sqhd", g_s, k, preferred_element_type=F32) * scale
    g_qkv = jnp.concatenate([merge(g_q), merge(g_k), merge(g_v)], axis=1).astype(BF16)
    return g_qkv, gbranch.astype(F32) + mm_nt(g_qkv, w_qkv)


def generic_total(seg_pairs, cross_pairs, small, planes, own):
    axes = ("row", "seg")
    me = lax.axis_index("seg")
    shards = [
        lax.psum_scatter(part, axes, scatter_dimension=0, tiled=True) for part in small_grads(*small, 1.0 / planes)
    ]

    def mine(values, dim):
        return lax.dynamic_slice_in_dim(values, me * own, own, dim)

    big = []
    for at in (6, 4, 0, 2):
        cross = mm(mine(cross_pairs[at], 1), mine(cross_pairs[at + 1], 0))
        both = jnp.concatenate([mm(seg_pairs[at], seg_pairs[at + 1]), cross], axis=0)
        big.append(lax.psum_scatter(both, axes, scatter_dimension=0, tiled=True))
    return big, shards


def per_device(
    tokens, doc_ids, w_qkv, w_out, w_up, w_down, biases, gains, b_up, pos_table, cotangent, *, sizes
):
    lines, planes = sizes
    row_count, local_length, width = tokens.shape
    seg_here = local_length // SEGLEN
    segments = doc_ids.shape[1]
    total = row_count * local_length
    own = row_count * seg_here
    cot = cotangent.reshape(total, width)
    (
        qkv, probs, n1, r1, slope, n2, r2, y, xt, mixedt, firstt, hiddent,
        ccls, gcls, csums, cbsums, gpos, cxt, cmixedt, cfirstt, chiddent, cgqkv, cgbranch, cginner, cgsecond,
    ) = forward_blocks(
        tokens.reshape(total, width), cot, w_qkv, w_out, w_up, w_down, biases, gains, b_up, doc_ids, pos_table, planes,
        tile=256 if planes <= 4 else 128,
    )
    output, gsecond, ginner, gbranch, sums, bsums = early_backward(
        gcls, ccls, cot, y, n2, r2, slope, n1, r1, w_up, w_down, gains
    )
    cross_pairs = (cfirstt, cginner, chiddent, cgsecond, cmixedt, cgbranch, cxt, cgqkv)
    share = 1.0 / planes
    if (lines, planes) == (8, 4) and total == 2048 and width == 16 * PART:
        *grads, small, gx = late_backward(
            (firstt, ginner, hiddent, gsecond, mixedt, gbranch, xt), cross_pairs, (sums, bsums, csums, cbsums, gpos), (qkv, probs, w_qkv, w_out), share
        )
        gx, *grads = finish(gx, grads)
        small = small.reshape(-1)
        index = lax.axis_index("row") * planes + lax.axis_index("seg")
        shards, start = [], 0
        for size in (12 * width, 4 * width, 8 * width, segments * width):
            count = size // (lines * planes)
            shards.append(lax.dynamic_slice_in_dim(small, start + index * count, count, 0))
            start += size
    else:
        gqkv, gx = attention_back(qkv, probs, gbranch, w_qkv[0], w_out[0])
        bias_sums = jnp.stack([jnp.sum(gqkv[:, at : at + width].astype(F32), axis=0) for at in (0, 2 * width)])
        grads, shards = generic_total(
            (firstt, ginner, hiddent, gsecond, mixedt, gbranch, xt, gqkv), cross_pairs, (sums, bsums, csums, cbsums, gpos, bias_sums), planes, own
        )
    return (output.reshape(tokens.shape), gx.reshape(tokens.shape), *grads, *shards)


def solution(mesh):
    sizes = (mesh.shape["row"], mesh.shape["seg"])
    tokens_at = P("row", "seg", None)
    return jax.shard_map(
        functools.partial(per_device, sizes=sizes),
        mesh=mesh,
        in_specs=(tokens_at, P("row", None)) + (P(),) * 8 + (tokens_at,),
        out_specs=(tokens_at, tokens_at) + (P(("row", "seg"), None),) * 4 + (P(("row", "seg")),) * 4,
        check_vma=False,
    )
```

profile of v0, /device:TPU:0, one launch (start us, length us, event | category | flops | bytes accessed | tf_op | source)
XLA Modules:
  0.0 222.0 jit_solution(16899773662482555526)
XLA Ops:
  0.6 70.1 %forward_blocks.1 = (bf16[3,2048,768]{2,1,0:T(8,128)(2,1)}, bf16[16,6,128,256]{3,2,1,0:T(8,128)(2,1)}, bf16[2048,768]{1,0:T(8,128)(2,1)}, f32[2048,128]{1,0:T(8,...) custom-call(bf16[2048,768]{1,0:T(8,128)(2,1)} %bitcast.16, ...), custom_call_target="tpu_custom_call" | custom-call | tf_op jit(solution)/shard_map/forward_blocks/pallas_call | solution.py:467
  70.7 34.9 %early_backward.1 = (bf16[2048,768]{1,0:T(8,128)(2,1)}, bf16[2048,768]{1,0:T(8,128)(2,1)}, bf16[2048,3072]{1,0:T(8,128)(2,1)}, bf16[2048,768]{1,0:T(8,128)(2,1)}...) custom-call(f32[16,768]{1,0:T(8,128)} %get-tuple-element.52.gcls_ref, f32[16,768]{1,0:T(8,128)} %get-tuple-element.53.ccls_ref, ...), custom_call_target="tpu_custom_call" | custom-call | tf_op jit(solution)/shard_map/early_backward/pallas_call | solution.py:639
  105.6 108.9 %late_backward.1 = (f32[48,2304]{1,0:T(8,128)}, f32[48,768]{1,0:T(8,128)}, f32[48,3072]{1,0:T(8,128)}, f32[192,768]{1,0:T(8,128)}, f32[32,768]{1,0:T(8,128)}, /*index=5*/bf16[2048,768]{1,0:T(8,128)(2,1)}) custom-call(bf16[2,2,4,48,2048]{4,3,2,1,0:T(8,128)(2,1)} %bitcast.19, bf16[2048,3072]{1,0:T(8,128)(2,1)} %get-tuple-element.62.ginner, ...), custom_call_target="tpu_custom_call" | custom-call | tf_op jit(solution)/shard_map/late_backward/pallas_call | solution.py:1237
  214.6 0.0 copy-start
  214.6 5.5 %finish.1 = (f32[2048,768]{1,0:T(8,128)}, f32[48,2304]{1,0:T(8,128)}, f32[48,768]{1,0:T(8,128)}, f32[48,3072]{1,0:T(8,128)}, f32[192,768]{1,0:T(8,128)}) custom-call(bf16[2048,768]{1,0:T(8,128)(2,1)} %get-tuple-element.83.gx_ref, f32[48,2304]{1,0:T(8,128)} %get-tuple-element.84.a_ref, f32[48,768]{1,0:T(8,128)} %get-tuple-element.85.b_ref, ...), custom_call_target="tpu_custom_call" | custom-call | tf_op jit(solution)/shard_map/finish/pallas_call | solution.py:1284
  220.1 0.0 copy-done
  220.1 0.6 fusion
  220.8 0.7 dynamic_slice.12
  221.4 0.6 dynamic_slice.13
  (1 shorter events, 0.0 us)
Async XLA Ops:
  214.6 5.5 %copy-start = (f32[32,768]{1,0:T(8,128)S(1)}, f32[32,768]{1,0:T(8,128)}, u32[]{:S(2)}) copy-start(f32[32,768]{1,0:T(8,128)} %get-tuple-element.93) | copy-start | bytes 294916
where the time goes:
time: 222 us
  Pallas kernels  219 us (99%)
    pallas_call x1, Pallas kernels, late_backward(): pl.pallas_call(functools.partial(late_kernel, share=share), in_specs=[any...  109 us
    pallas_call x1, Pallas kernels, forward_blocks(): pl.pallas_call(functools.partial(forward_kernel, ff_chunk=ff_chunk, devic...  70.1 us
    pallas_call x1, Pallas kernels, early_backward(): pl.pallas_call(functools.partial(early_kernel, ff_chunk=ff_chunk), grid=(...  34.9 us
    pallas_call x1, Pallas kernels, finish(): pl.pallas_call(finish_kernel, grid=(total // tile,), in_specs=[rows] + he...  5.51 us

commit v1 on v0

--- a/solution.py
+++ b/solution.py
@@ -103,7 +103,7 @@
     return onehot, key[:rows] == keys_across
 
 
-def cross_part(me, doc_ref, table_ref, bias_ref, gain_ref, bup_ref, outs, writes, weights, copies, scratch, ff_chunk):
+def cross_part(me, onehot, allowed, embed, bias_ref, gain_ref, bup_ref, outs, writes, weights, copies, scratch, ff_chunk):
     (
         ccls_ref, gcls_ref, sums_ref, bsums_ref, gpos_ref, xt_ref, mixedt_ref, firstt_ref, hiddent_ref,
         gqkv_ref, gbranch_ref, ginner_ref, gsecond_ref,
@@ -116,8 +116,6 @@
     bias = bias_ref[...].astype(F32)[:, 1]
     gain = gain_ref[1].astype(F32)
     up_bias = bup_ref[1:2, :].astype(F32)
-    onehot, allowed = places(doc_ref[...], rows, own, table_ref.shape[0])
-    embed = mm(onehot.astype(BF16), table_ref[...])
     x = (whole_ref[0] + embed).astype(BF16)
     gy = whole_ref[1]
     xt_ref[...] = turned(x)
@@ -415,10 +413,12 @@
         packed[1] = cls_ref[...].astype(BF16)
         for send in sends(1):
             send.start()
+        onehot, allowed = places(doc_ref[...], own * devices, own, table_ref.shape[0])
+        embed = mm(onehot.astype(BF16), table_ref[...])
         arrived(0, cross_scratch[-1])
         arrived(1, cross_scratch[-1])
         cross_part(
-            me, doc_ref, table_ref, bias_ref, gain_ref, bup_ref, outs, writes,
+            me, onehot, allowed, embed, bias_ref, gain_ref, bup_ref, outs, writes,
             cross_weights, cross_copies, cross_scratch, ff_chunk,
         )
 
@@ -668,7 +668,7 @@
     ("b", 8, 14, 17, 20, 24), ("a", 8, 14, 17, 20, 24), ("b", 11, 17, 20, 23, 26), ("a", 11, 17, 20, 23, 26),
     ("b", 14, 18, 21, 23, 26), ("a", 19, 23, 25, 27, 28), ("b", 24, 26, 27, 28, 28), ("a", 24, 26, 27, 28, 28),
 )
-SMALL_MOMENTS = (1, 4, 6, 8, 10, 12)
+SMALL_MOMENTS = (1, 3, 5, 7, 10, 13)
 SMALL_LATE = (23, 24, 25, 26, 27, 28)
 WAYS = "".join(row[0] for row in CHAIN_TABLE)
 

time: 222 us -> 220 us (level)
  no operation moved by 1% of the time
where the time goes in v1:
time: 220 us
  Pallas kernels  218 us (99%)
    pallas_call x1, Pallas kernels, late_backward(): pl.pallas_call(functools.partial(late_kernel, share=share), in_specs=[any...  107 us
    pallas_call x1, Pallas kernels, forward_blocks(): pl.pallas_call(functools.partial(forward_kernel, ff_chunk=ff_chunk, devic...  69.7 us
    pallas_call x1, Pallas kernels, early_backward(): pl.pallas_call(functools.partial(early_kernel, ff_chunk=ff_chunk), grid=(...  34.9 us
    pallas_call x1, Pallas kernels, finish(): pl.pallas_call(finish_kernel, grid=(total // tile,), in_specs=[rows] + he...  5.51 us

profile of v1, /device:TPU:0, one launch (start us, length us, event | category | flops | bytes accessed | tf_op | source)
XLA Modules:
  0.0 220.1 jit_solution(753462161047538981)
XLA Ops:
  0.6 69.7 %forward_blocks.1 = (bf16[3,2048,768]{2,1,0:T(8,128)(2,1)}, bf16[16,6,128,256]{3,2,1,0:T(8,128)(2,1)}, bf16[2048,768]{1,0:T(8,128)(2,1)}, f32[2048,128]{1,0:T(8,...) custom-call(bf16[2048,768]{1,0:T(8,128)(2,1)} %bitcast.16, ...), custom_call_target="tpu_custom_call" | custom-call | tf_op jit(solution)/shard_map/forward_blocks/pallas_call | solution.py:467
  70.4 34.9 %early_backward.1 = (bf16[2048,768]{1,0:T(8,128)(2,1)}, bf16[2048,768]{1,0:T(8,128)(2,1)}, bf16[2048,3072]{1,0:T(8,128)(2,1)}, bf16[2048,768]{1,0:T(8,128)(2,1)}...) custom-call(f32[16,768]{1,0:T(8,128)} %get-tuple-element.52.gcls_ref, f32[16,768]{1,0:T(8,128)} %get-tuple-element.53.ccls_ref, ...), custom_call_target="tpu_custom_call" | custom-call | tf_op jit(solution)/shard_map/early_backward/pallas_call | solution.py:639
  105.3 107.4 %late_backward.1 = (f32[48,2304]{1,0:T(8,128)}, f32[48,768]{1,0:T(8,128)}, f32[48,3072]{1,0:T(8,128)}, f32[192,768]{1,0:T(8,128)}, f32[32,768]{1,0:T(8,128)}, /*index=5*/bf16[2048,768]{1,0:T(8,128)(2,1)}) custom-call(bf16[2,2,4,48,2048]{4,3,2,1,0:T(8,128)(2,1)} %bitcast.19, bf16[2048,3072]{1,0:T(8,128)(2,1)} %get-tuple-element.62.ginner, ...), custom_call_target="tpu_custom_call" | custom-call | tf_op jit(solution)/shard_map/late_backward/pallas_call | solution.py:1237
  212.7 0.0 copy-start
  212.7 5.5 %finish.1 = (f32[2048,768]{1,0:T(8,128)}, f32[48,2304]{1,0:T(8,128)}, f32[48,768]{1,0:T(8,128)}, f32[48,3072]{1,0:T(8,128)}, f32[192,768]{1,0:T(8,128)}) custom-call(bf16[2048,768]{1,0:T(8,128)(2,1)} %get-tuple-element.83.gx_ref, f32[48,2304]{1,0:T(8,128)} %get-tuple-element.84.a_ref, f32[48,768]{1,0:T(8,128)} %get-tuple-element.85.b_ref, ...), custom_call_target="tpu_custom_call" | custom-call | tf_op jit(solution)/shard_map/finish/pallas_call | solution.py:1284
  218.2 0.0 copy-done
  218.2 0.6 fusion
  218.9 0.7 dynamic_slice.12
  219.5 0.6 dynamic_slice.13
  (1 shorter events, 0.0 us)
Async XLA Ops:
  212.7 5.5 %copy-start = (f32[32,768]{1,0:T(8,128)S(1)}, f32[32,768]{1,0:T(8,128)}, u32[]{:S(2)}) copy-start(f32[32,768]{1,0:T(8,128)} %get-tuple-element.93) | copy-start | bytes 294916
